TPU v7x, 32 devices: a whole 2x2x4 slice. The times are simulated.
32 devices in a mesh: groups: 2 (over x), ia: 16 (over z, y, core).
Axes of the slice: x: 2, y: 2, z: 4, core: 2. Of those that a mesh axis runs over, the one named last changes fastest.
Arguments:
- pair: bfloat16 [512, 256, 128], P(('groups', 'ia')), parts along dimension 0, may hold values from -6 to 6
- pad_mask: int32 [512], P('groups'), parts along dimension 0, may hold values 0 or 1
- w_in: bfloat16 [128, 640], replicated, may hold values from -0.5 to 0.5
- in_exps: int32 [20], replicated, may hold values from -1 to 1
- w_out: bfloat16 [128, 128], replicated, may hold values from -0.5 to 0.5
- out_exps: int32 [4], replicated, may hold values from -1 to 1, as said below
- in_gain: float32 [128], replicated, may hold values from 0.1 to 1.9
- in_bias: float32 [128], replicated, may hold values from -3 to 3
- out_gain: float32 [128], replicated, may hold values from 0.1 to 1.9
- out_bias: float32 [128], replicated, may hold values from -3 to 3
Outputs:
- update: bfloat16 [512, 256, 128], P(('groups', 'ia')), parts along dimension 0
There are 2 independent parts, one for each index of `groups`. A program takes and returns all parts, laid end to end along the dimension named above; an argument that names none is the same for every part. Nothing has to cross between parts.
Inputs may be any that keep to these rules, and one draw needn't show every extreme that they name: `out_exps`: power-of-two exponents of the output projection's column blocks.
All inputs are finite; a program needn't handle non-finite values.
Results may differ from a plain program's by a relative error of at most 0.0085.
Values may be sent and summed in bfloat16 or wider, within the bound.
A program may use at most 128 MiB of HBM per device.

v0:
```python
import jax
import jax.numpy as jnp
from jax import lax
from jax.sharding import PartitionSpec as P

BLK = 32


def layer_norm(values, gain, bias, axis):
    mean_val = jnp.mean(values, axis=axis, keepdims=True)
    centred = values - mean_val
    variance = jnp.mean(centred * centred, axis=axis, keepdims=True)
    return centred * lax.rsqrt(variance + 1e-05) * gain + bias


def scaled_weight(weight, exponents):
    factor = jnp.repeat(jnp.exp2(exponents.astype(jnp.float32)), BLK)
    return (weight.astype(jnp.float32) * factor[None, :]).astype(jnp.bfloat16)


def shards(pair, pad_mask, w_in, in_exps, w_out, out_exps, in_gain, in_bias, out_gain, out_bias):
    tok_rows = pair.shape[0]
    whole_len = pair.shape[1]
    width_in = pair.shape[2]
    hidden = w_out.shape[0]
    row_start = lax.axis_index("ia") * tok_rows
    w_eff = scaled_weight(w_in, in_exps)
    w_last = scaled_weight(w_out, out_exps)
    mask_f = pad_mask.astype(jnp.float32)
    mask_rows = lax.dynamic_slice_in_dim(mask_f, row_start, tok_rows, 0)
    normed = layer_norm(pair.astype(jnp.float32), in_gain, in_bias, -1).astype(jnp.bfloat16)
    proj = jnp.dot(
        normed.reshape(tok_rows * whole_len, width_in), w_eff, preferred_element_type=jnp.float32
    )
    proj = proj.reshape(tok_rows, whole_len, 5 * hidden)
    pair_mask = mask_rows[:, None, None] * mask_f[None, :, None]
    left = (
        jax.nn.sigmoid(proj[:, :, 0:hidden]) * proj[:, :, hidden : 2 * hidden] * pair_mask
    ).astype(jnp.bfloat16)
    right = (
        jax.nn.sigmoid(proj[:, :, 2 * hidden : 3 * hidden])
        * proj[:, :, 3 * hidden : 4 * hidden]
        * pair_mask
    ).astype(jnp.bfloat16)
    gate = jax.nn.sigmoid(proj[:, :, 4 * hidden : 5 * hidden]).astype(jnp.bfloat16)
    left_t = jnp.transpose(left, (2, 0, 1))
    right_t = jnp.transpose(right, (2, 0, 1))
    left_chan, right_chan = (
        lax.all_to_all(left_t, "ia", split_axis=0, concat_axis=1, tiled=True),
        lax.all_to_all(right_t, "ia", split_axis=0, concat_axis=1, tiled=True),
    )
    gate_moved = lax.all_to_all(gate, "ia", split_axis=1, concat_axis=0, tiled=True)
    gate_cols = jnp.swapaxes(gate_moved, 0, 1)
    tri_t = jnp.einsum(
        "hjk,hik->hji", right_chan, left_chan, preferred_element_type=jnp.float32
    ).astype(jnp.bfloat16)
    tri_cols = lax.all_to_all(tri_t, "ia", split_axis=1, concat_axis=0, tiled=True)
    tri_norm = layer_norm(
        tri_cols.astype(jnp.float32), out_gain[:, None, None], out_bias[:, None, None], 0
    ).astype(jnp.bfloat16)
    mixed = jnp.einsum("hji,hc->jic", tri_norm, w_last, preferred_element_type=jnp.float32)
    return (mixed * gate_cols.astype(jnp.float32)).astype(jnp.bfloat16)


def solution(mesh):
    return jax.shard_map(
        shards,
        mesh=mesh,
        in_specs=(
            P(("groups", "ia"), None, None),
            P("groups"),
            P(),
            P(),
            P(),
            P(),
            P(),
            P(),
            P(),
            P(),
        ),
        out_specs=P(("groups", "ia"), None, None),
        check_vma=False,
    )
```

profile of v0, /device:TPU:0, one launch (start us, length us, event | category | flops | bytes accessed | tf_op | source)
XLA Modules:
  0.0 135.6 jit_solution(7624923190836558820)
XLA Ops:
  0.0 0.0 copy-start.7
  0.0 0.0 copy-start.1
  0.0 0.0 copy-start.4
  0.0 0.8 convert_element_type.83
  0.8 0.1 dynamic_slice.3
  0.9 0.1 broadcast_multiply_fusion
  0.9 1.6 %convert_reduce_fusion = f32[16,256]{1,0:T(8,128)S(1)} fusion(bf16[16,256,128]{2,1,0:T(8,128)(2,1)} %param.10), kind=kLoop, calls=%fused_computation.1 | loop fusion | flops 1044480 | bytes 1064960 | tf_op jit(solution)/shard_map/reduce_sum | solution.py:10
  2.5 2.3 %fusion.2 = f32[16,256]{1,0:T(8,128)S(1)} fusion(bf16[16,256,128]{2,1,0:T(8,128)(2,1)} %param.10, f32[16,256]{1,0:T(8,128)S(1)} %broadcast_multiply_fusion.2), kind=kLoop, calls=%fused_computation.4 | loop fusion | flops 2093056 | bytes 1081344 | tf_op jit(solution)/shard_map/reduce_sum | solution.py:12
  4.9 0.0 copy-done.7
  4.9 0.1 broadcast_in_dim.4
  5.0 0.1 mul.108
  5.1 0.0 copy-done
  5.1 0.0 copy-done.1
  5.1 0.0 copy-done.4
  5.1 0.0 copy-done.3
  5.1 1.8 %fusion.26 = f32[16,256,640]{2,1,0:T(8,128)S(1)} fusion(bf16[16,256,128]{2,1,0:T(8,128)(2,1)S(1)} %copy-done, f32[128]{0:T(128)S(1)} %copy-done.3, f32[128]{0:T(128)S(1)} %copy-done.4, f32[16,256]{1,0:T(8,128)S(1)} %add_rsqrt_fusion.1, f32[16,256]{1,0:T(8,128)S(1)} %broadcast_multiply_fusion.2, bf16[128,640]{1,0:T(8,128)(2,1)S(1)} %copy-done.1, ...), kind=kOutput, calls=%fused_computation.38 | convolution fusion | flops 674480128 | bytes 11734528 | tf_op jit(solution)/shard_map/dot_general | solution.py:32
  6.9 2.0 %fusion.34 = (bf16[128,16,256]{0,2,1:T(8,128)(2,1)S(1)}, bf16[128,16,256]{0,2,1:T(8,128)(2,1)S(1)}, bf16[16,256,128]{2,1,0:T(8,128)(2,1)S(1)}) fusion(f32[16,256]{1,0:T(8,128)S(1)} %broadcast_multiply_fusion, f32[16,256,640]{2,1,0:T(8,128)S(1)} %fusion.26), kind=kLoop, calls=%fused_computation.45 | loop fusion | flops 8388608 | bytes 13647872 | tf_op jit(solution)/shard_map/transpose | solution.py:46
  8.9 1.7 %copy.30 = bf16[128,16,256]{2,1,0:T(8,128)(2,1)} copy(bf16[128,16,256]{0,2,1:T(8,128)(2,1)S(1)} %get-tuple-element.6) | data formatting | bytes 2097152 | tf_op jit(solution)/shard_map/transpose | solution.py:47
  10.6 7.4 %all-to-all-start = ((bf16[128,16,256]{2,1,0:T(8,128)(2,1)}), bf16[128,16,256]{2,1,0:T(8,128)(2,1)S(1)}, u32[]{:S(2)}, u32[]{:S(2)}) async-start(bf16[128,16,256]{2,1,0:T(8,128)(2,1)} %copy.30), calls=%async_computation | async-start | bytes 2097152 | tf_op jit(solution)/shard_map/all_to_all | solution.py:50
  18.0 1.7 %copy.32 = bf16[128,16,256]{2,1,0:T(8,128)(2,1)} copy(bf16[128,16,256]{0,2,1:T(8,128)(2,1)S(1)} %get-tuple-element.5) | data formatting | bytes 2097152 | tf_op jit(solution)/shard_map/transpose | solution.py:46
  19.7 21.2 %all-to-all-done = bf16[128,16,256]{2,1,0:T(8,128)(2,1)S(1)} async-done(((bf16[128,16,256]{2,1,0:T(8,128)(2,1)}), bf16[128,16,256]{2,1,0:T(8,128)(2,1)S(1)}, u32[]{:S(2)}, u32[]{:S(2)}) %all-to-all-start) | async-done | bytes 1048608 | tf_op jit(solution)/shard_map/all_to_all | solution.py:50
  40.9 6.9 %all-to-all-start.1 = ((bf16[128,16,256]{2,1,0:T(8,128)(2,1)}), bf16[128,16,256]{2,1,0:T(8,128)(2,1)S(1)}, u32[]{:S(2)}, u32[]{:S(2)}) async-start(bf16[128,16,256]{2,1,0:T(8,128)(2,1)} %copy.32), calls=%async_computation.1 | async-start | bytes 2097152 | tf_op jit(solution)/shard_map/all_to_all | solution.py:49
  47.8 1.6 %copy.38 = bf16[16,256,128]{2,0,1:T(8,128)(2,1)} copy(bf16[16,256,128]{2,1,0:T(8,128)(2,1)S(1)} %get-tuple-element.7) | data formatting | bytes 2097152 | tf_op jit(solution)/shard_map/convert_element_type | solution.py:45
  49.4 21.3 %all-to-all-done.1 = bf16[128,16,256]{2,1,0:T(8,128)(2,1)S(1)} async-done(((bf16[128,16,256]{2,1,0:T(8,128)(2,1)}), bf16[128,16,256]{2,1,0:T(8,128)(2,1)S(1)}, u32[]{:S(2)}, u32[]{:S(2)}) %all-to-all-start.1) | async-done | bytes 1048608 | tf_op jit(solution)/shard_map/all_to_all | solution.py:49
  70.7 6.9 %all-to-all-start.3 = ((bf16[16,256,128]{2,0,1:T(8,128)(2,1)}), bf16[16,256,128]{2,0,1:T(8,128)(2,1)S(1)}, u32[]{:S(2)}, u32[]{:S(2)}) async-start(bf16[16,256,128]{2,0,1:T(8,128)(2,1)} %copy.38), calls=%async_computation.3 | async-start | bytes 2097152 | tf_op jit(solution)/shard_map/all_to_all | solution.py:52
  77.6 0.1 copy.31
  77.7 0.1 copy.33
  77.8 0.5 convolution_convert_fusion
  78.3 0.0 copy-start.8
  78.3 1.6 %copy.34 = bf16[8,256,256]{2,0,1:T(8,128)(2,1)} copy(bf16[8,256,256]{2,1,0:T(8,128)(2,1)S(1)} %convolution_convert_fusion) | data formatting | bytes 2097152 | tf_op jit(solution)/shard_map/convert_element_type | solution.py:56
  79.9 20.6 %all-to-all-done.3 = bf16[16,256,128]{2,0,1:T(8,128)(2,1)S(1)} async-done(((bf16[16,256,128]{2,0,1:T(8,128)(2,1)}), bf16[16,256,128]{2,0,1:T(8,128)(2,1)S(1)}, u32[]{:S(2)}, u32[]{:S(2)}) %all-to-all-start.3) | async-done | bytes 1048608 | tf_op jit(solution)/shard_map/all_to_all | solution.py:52
  100.5 6.9 %all-to-all-start.2 = ((bf16[8,256,256]{2,0,1:T(8,128)(2,1)}), bf16[8,256,256]{2,0,1:T(8,128)(2,1)}, u32[]{:S(2)}, u32[]{:S(2)}) async-start(bf16[8,256,256]{2,0,1:T(8,128)(2,1)} %copy.34), calls=%async_computation.2 | async-start | bytes 2097152 | tf_op jit(solution)/shard_map/all_to_all | solution.py:57
  107.5 0.0 copy-done.8
  107.5 0.1 broadcast_in_dim.5
  107.6 0.1 mul.125
  107.6 0.2 copy.39
  107.9 22.6 %all-to-all-done.2 = bf16[8,256,256]{2,0,1:T(8,128)(2,1)} async-done(((bf16[8,256,256]{2,0,1:T(8,128)(2,1)}), bf16[8,256,256]{2,0,1:T(8,128)(2,1)}, u32[]{:S(2)}, u32[]{:S(2)}) %all-to-all-start.2) | async-done | bytes 1048608 | tf_op jit(solution)/shard_map/all_to_all | solution.py:57
  130.5 1.5 %fusion.41 = (bf16[8,256,256]{2,1,0:T(8,128)(2,1)S(1)}, f32[16,8,16,256]{3,2,0,1:T(8,128)S(1)}) fusion(bf16[8,256,256]{2,0,1:T(8,128)(2,1)} %all-to-all-done.2), kind=kLoop, calls=%fused_computation.59 | loop fusion | flops 524288 | bytes 4194304 | tf_op jit(solution)/shard_map/all_to_all | solution.py:57
  132.0 0.2 fusion.25
  132.2 0.3 multiply_reduce_fusion
  132.5 0.0 copy-start.5
  132.6 0.0 copy-start.6
  132.6 0.2 copy.36
  132.8 0.4 copy-done.5
  133.2 0.0 copy-done.6
  133.2 0.4 fusion.23
  133.6 0.4 copy-done.2
  134.0 1.6 %fusion.19 = bf16[16,256,128]{2,1,0:T(8,128)(2,1)} fusion(f32[16,16,16,128]{3,0,1,2:T(8,128)S(1)} %copy.39, bf16[128,16,256]{2,1,0:T(8,128)(2,1)S(1)} %fusion.23, bf16[128,128]{1,0:T(8,128)(2,1)S(1)} %copy-done.2, f32[128]{0:T(128)S(1)} %mul.125), kind=kOutput, calls=%fused_computation.27 | convolution fusion | flops 135315456 | bytes 4227584 | tf_op jit(solution)/shard_map/hji,hc->jic/dot_general | solution.py:61
  (9 shorter events, 0.0 us)
Async XLA Ops:
  0.0 5.1 %copy-start = (bf16[16,256,128]{2,1,0:T(8,128)(2,1)S(1)}, bf16[16,256,128]{2,1,0:T(8,128)(2,1)}, u32[]{:S(2)}) copy-start(bf16[16,256,128]{2,1,0:T(8,128)(2,1)} %param.10) | copy-start | bytes 3145732
  0.0 4.9 %copy-start.7 = (s32[20]{0:T(128)S(1)}, s32[20]{0:T(128)}, u32[]{:S(2)}) copy-start(s32[20]{0:T(128)} %param.13) | copy-start | bytes 244
  0.0 5.1 %copy-start.1 = (bf16[128,640]{1,0:T(8,128)(2,1)S(1)}, bf16[128,640]{1,0:T(8,128)(2,1)}, u32[]{:S(2)}) copy-start(bf16[128,640]{1,0:T(8,128)(2,1)} %param.12) | copy-start | bytes 491524
  0.0 5.1 %copy-start.4 = (f32[128]{0:T(128)S(1)}, f32[128]{0:T(128)}, u32[]{:S(2)}) copy-start(f32[128]{0:T(128)} %param.16) | copy-start | bytes 1540
  0.0 5.1 %copy-start.3 = (f32[128]{0:T(128)S(1)}, f32[128]{0:T(128)}, u32[]{:S(2)}) copy-start(f32[128]{0:T(128)} %param.17) | copy-start | bytes 1540
  10.6 30.3 %all-to-all-start = ((bf16[128,16,256]{2,1,0:T(8,128)(2,1)}), bf16[128,16,256]{2,1,0:T(8,128)(2,1)S(1)}, u32[]{:S(2)}, u32[]{:S(2)}) async-start(bf16[128,16,256]{2,1,0:T(8,128)(2,1)} %copy.30), calls=%async_computation | async-start | bytes 2097152 | tf_op jit(solution)/shard_map/all_to_all | solution.py:50
  40.9 29.8 %all-to-all-start.1 = ((bf16[128,16,256]{2,1,0:T(8,128)(2,1)}), bf16[128,16,256]{2,1,0:T(8,128)(2,1)S(1)}, u32[]{:S(2)}, u32[]{:S(2)}) async-start(bf16[128,16,256]{2,1,0:T(8,128)(2,1)} %copy.32), calls=%async_computation.1 | async-start | bytes 2097152 | tf_op jit(solution)/shard_map/all_to_all | solution.py:49
  70.7 29.8 %all-to-all-start.3 = ((bf16[16,256,128]{2,0,1:T(8,128)(2,1)}), bf16[16,256,128]{2,0,1:T(8,128)(2,1)S(1)}, u32[]{:S(2)}, u32[]{:S(2)}) async-start(bf16[16,256,128]{2,0,1:T(8,128)(2,1)} %copy.38), calls=%async_computation.3 | async-start | bytes 2097152 | tf_op jit(solution)/shard_map/all_to_all | solution.py:52
  78.3 29.2 %copy-start.8 = (s32[4]{0:T(128)S(1)}, s32[4]{0:T(128)}, u32[]{:S(2)}) copy-start(s32[4]{0:T(128)} %param.15) | copy-start | bytes 52
  100.5 29.9 %all-to-all-start.2 = ((bf16[8,256,256]{2,0,1:T(8,128)(2,1)}), bf16[8,256,256]{2,0,1:T(8,128)(2,1)}, u32[]{:S(2)}, u32[]{:S(2)}) async-start(bf16[8,256,256]{2,0,1:T(8,128)(2,1)} %copy.34), calls=%async_computation.2 | async-start | bytes 2097152 | tf_op jit(solution)/shard_map/all_to_all | solution.py:57
  132.5 0.7 copy-start.5
  132.6 0.7 copy-start.6
  133.2 0.8 copy-start.2
where the time goes:
time: 137 us; the launch traced here: 136 us
  waiting for transfers between devices  85.8 us (63%)
  starting transfers between devices  28 us (20%)
  other arithmetic  9.18 us (7%)
  local copies, waits for them, and re-layouts  8.48 us (6%)
  matrix products  3.88 us (3%)
    all_to_all x1, waiting for transfers between devices, shards(): lax.all_to_all(tri_t, 'ia', split_axis=1, concat_axis=0, tiled=True)  22.6 us
    all_to_all x1, waiting for transfers between devices, shards(): lax.all_to_all(left_t, 'ia', split_axis=0, concat_axis=1, tiled=True)  21.3 us
    all_to_all x1, waiting for transfers between devices, shards(): lax.all_to_all(right_t, 'ia', split_axis=0, concat_axis=1, tiled=True)  21.2 us
    all_to_all x1, waiting for transfers between devices, shards(): lax.all_to_all(gate, 'ia', split_axis=1, concat_axis=0, tiled=True)  20.6 us
    all_to_all x1, starting transfers between devices, shards(): lax.all_to_all(right_t, 'ia', split_axis=0, concat_axis=1, tiled=True)  7.4 us
    all_to_all x1, starting transfers between devices, shards(): lax.all_to_all(tri_t, 'ia', split_axis=1, concat_axis=0, tiled=True)  6.92 us
    all_to_all x1, starting transfers between devices, shards(): lax.all_to_all(gate, 'ia', split_axis=1, concat_axis=0, tiled=True)  6.86 us
    all_to_all x1, starting transfers between devices, shards(): lax.all_to_all(left_t, 'ia', split_axis=0, concat_axis=1, tiled=True)  6.86 us
  transfers between devices with their start and end apart: 4, of which 4 were waited for; matrix products, arithmetic and copies ran while one was open for 4% of the time, Pallas kernels for 0%

commit v1 on v0

--- a/solution.py
+++ b/solution.py
@@ -1,6 +1,10 @@
+import functools
+
 import jax
 import jax.numpy as jnp
 from jax import lax
+from jax.experimental import pallas as pl
+from jax.experimental.pallas import tpu as pltpu
 from jax.sharding import PartitionSpec as P
 
 BLK = 32
@@ -62,9 +66,105 @@
     return (mixed * gate_cols.astype(jnp.float32)).astype(jnp.bfloat16)
 
 
+CORE, Y, Z, HALF = 1, 2, 4, 8
+CHIPS = (0, Z, Y, Z | Y)
+
+
+def gated(normed, weight, mask):
+    hidden = weight.shape[1] // 2
+    rows, cols, width = normed.shape
+    proj = jnp.dot(normed.reshape(rows * cols, width), weight, preferred_element_type=jnp.float32)
+    proj = proj.reshape(rows, cols, 2 * hidden)
+    value = (jax.nn.sigmoid(proj[:, :, :hidden]) * proj[:, :, hidden:] * mask).astype(jnp.bfloat16)
+    return jnp.transpose(value, (2, 0, 1))
+
+
+def place(rows, *refs):
+    me = lax.axis_index("ia")
+    out_ref = refs[-1]
+    at = 0
+    for far in (0, HALF):
+        for chip in CHIPS:
+            for core in (0, CORE):
+                start = pl.multiple_of((me ^ (far | chip | core)) * rows, rows)
+                out_ref[:, pl.ds(start, rows), :] = refs[at][:, core * rows : (core + 1) * rows, :]
+            at += 1
+
+
+def half_shards(
+    count, pair, pad_mask, w_in, in_exps, w_out, out_exps, in_gain, in_bias, out_gain, out_bias
+):
+    rows, whole_len, _ = pair.shape
+    hidden = w_out.shape[0]
+    me = lax.axis_index("ia")
+
+    def swap(array, bits):
+        return lax.ppermute(array, "ia", [(at, at ^ bits) for at in range(count)])
+
+    w_eff = scaled_weight(w_in, in_exps)
+    w_last = scaled_weight(w_out, out_exps)
+    mask_f = pad_mask.astype(jnp.float32)
+
+    def pair_mask(owner):
+        own = lax.dynamic_slice_in_dim(mask_f, owner * rows, rows, 0)
+        return own[:, None, None] * mask_f[None, :, None]
+
+    def norm_in(values):
+        return layer_norm(values.astype(jnp.float32), in_gain, in_bias, -1).astype(jnp.bfloat16)
+
+    def gates(normed):
+        parts = [
+            lax.dynamic_slice_in_dim(normed, (me ^ core ^ chip) * rows, rows, 1)
+            for core in (0, CORE)
+            for chip in CHIPS
+        ]
+        picked = jnp.concatenate(parts, 1)
+        proj = jnp.dot(
+            picked.reshape(-1, picked.shape[2]),
+            w_eff[:, 4 * hidden :],
+            preferred_element_type=jnp.float32,
+        )
+        gate = jax.nn.sigmoid(proj).astype(jnp.bfloat16).reshape(rows, 2, 4 * rows, hidden)
+        return gate[:, 0], gate[:, 1]
+
+    pair_far = swap(pair, HALF)
+    normed = norm_in(pair)
+    right = gated(normed, w_eff[:, 2 * hidden : 4 * hidden], pair_mask(me))
+    right_z = swap(right, Z)
+    right_y = swap(right, Y)
+    right_zy = swap(right_z, Y)
+    rights = jnp.concatenate([right, right_z, right_y, right_zy], 1)
+
+    def finish(normed_rows, owner):
+        left = gated(normed_rows, w_eff[:, : 2 * hidden], pair_mask(owner))
+        gate_mine, gate_other = gates(normed_rows)
+        lefts = jnp.concatenate([left, swap(left, CORE)], 1)
+        gate = jnp.concatenate([gate_mine, swap(gate_other, CORE)], 0)
+        tri = jnp.einsum(
+            "hjk,hik->hji", rights, lefts, preferred_element_type=jnp.float32
+        ).astype(jnp.bfloat16)
+        tri_norm = layer_norm(
+            tri.astype(jnp.float32), out_gain[:, None, None], out_bias[:, None, None], 0
+        ).astype(jnp.bfloat16)
+        mixed = jnp.einsum("hji,hc->jic", tri_norm, w_last, preferred_element_type=jnp.float32)
+        update = (mixed * jnp.swapaxes(gate, 0, 1).astype(jnp.float32)).astype(jnp.bfloat16)
+        blocks = [update[at * rows : (at + 1) * rows] for at in range(4)]
+        return [blocks[0]] + [swap(block, chip) for block, chip in zip(blocks[1:], CHIPS[1:])]
+
+    pieces = finish(normed, me) + finish(norm_in(pair_far), me ^ HALF)
+    return pl.pallas_call(
+        functools.partial(place, rows),
+        out_shape=jax.ShapeDtypeStruct(pair.shape, jnp.bfloat16),
+        in_specs=[pl.BlockSpec(memory_space=pltpu.VMEM)] * len(pieces),
+        out_specs=pl.BlockSpec(memory_space=pltpu.VMEM),
+    )(*pieces)
+
+
 def solution(mesh):
+    count = mesh.shape["ia"]
+    body = functools.partial(half_shards, count) if count == 16 else shards
     return jax.shard_map(
-        shards,
+        body,
         mesh=mesh,
         in_specs=(
             P(("groups", "ia"), None, None),

time: 137 us -> 148 us (1.080)
  local copies, waits for them, and re-layouts: 8.48 us -> 24.1 us
  waiting for transfers between devices: 85.8 us -> 71.2 us
  other arithmetic: 9.18 us -> 22.7 us
  starting transfers between devices: 28 us -> 15.8 us
  matrix products: 3.88 us -> 10.2 us
  Pallas kernels: 0 us -> 2.38 us
    all_to_all x4 -> x0, waiting for transfers between devices: 85.8 us -> none  [the longest x1 22.6 us: shards(): lax.all_to_all(tri_t, 'ia', split_axis=1, concat_axis=0, tiled=True)]
    ppermute x0 -> x14, waiting for transfers between devices: none -> 71.2 us  [swap(): return lax.ppermute(array, 'ia', [(at, at ^ bits) for at in range(count)])]
    all_to_all x4 -> x0, starting transfers between devices: 28 us -> none  [the longest x1 7.4 us: shards(): lax.all_to_all(right_t, 'ia', split_axis=0, concat_axis=1, tiled=True)]
    ppermute x0 -> x14, starting transfers between devices: none -> 15.8 us  [swap(): return lax.ppermute(array, 'ia', [(at, at ^ bits) for at in range(count)])]
    concatenate x0 -> x5, local copies, waits for them, and re-layouts: none -> 14.9 us  [the longest x2 7.99 us: finish(): lefts = jnp.concatenate([left, swap(left, CORE)], 1)]
    concatenate x0 -> x3, other arithmetic: none -> 8.05 us  [the longest x2 4.27 us: finish(): lefts = jnp.concatenate([left, swap(left, CORE)], 1)]
    dot_general x3 -> x9, matrix products: 3.88 us -> 10.2 us  [the longest x2 4.77 us: finish(): jnp.einsum('hjk,hik->hji', rights, lefts, preferred_element_type=jnp.floa...]
    unnamed x18 -> x49, local copies, waits for them, and re-layouts: 0.82 us -> 4.33 us
  transfers between devices with their start and end apart: 4 -> 14, of which waited for: 4 -> 6; matrix products, arithmetic and copies ran while one was open for 4% -> 33% of each run, Pallas kernels for 0% -> 0%
where the time goes in v1:
time: 148 us; the launch traced here: 147 us
  waiting for transfers between devices  71.2 us (48%)
  local copies, waits for them, and re-layouts  24.1 us (16%)
  other arithmetic  22.7 us (15%)
  starting transfers between devices  15.8 us (11%)
  matrix products  10.2 us (7%)
  Pallas kernels  2.38 us (2%)
    ppermute x14, waiting for transfers between devices, swap(): return lax.ppermute(array, 'ia', [(at, at ^ bits) for at in range(count)])  71.2 us
    ppermute x14, starting transfers between devices, swap(): return lax.ppermute(array, 'ia', [(at, at ^ bits) for at in range(count)])  15.8 us
    concatenate x2, local copies, waits for them, and re-layouts, finish(): lefts = jnp.concatenate([left, swap(left, CORE)], 1)  7.99 us
    concatenate x1, local copies, waits for them, and re-layouts, half_shards(): rights = jnp.concatenate([right, right_z, right_y, right_zy], 1)  6.84 us
    dot_general x2, matrix products, finish(): jnp.einsum('hjk,hik->hji', rights, lefts, preferred_element_type=jnp.floa...  4.77 us
    reduce_sum x4, other arithmetic, layer_norm(): variance = jnp.mean(centred * centred, axis=axis, keepdims=True)  4.39 us
    unnamed x49, local copies, waits for them, and re-layouts  4.33 us
    concatenate x2, other arithmetic, finish(): lefts = jnp.concatenate([left, swap(left, CORE)], 1)  4.27 us
  transfers between devices with their start and end apart: 14, of which 6 were waited for; matrix products, arithmetic and copies ran while one was open for 33% of the time, Pallas kernels for 0%

profile of v1, /device:TPU:0, one launch (start us, length us, event | category | flops | bytes accessed | tf_op | source)
XLA Modules:
  0.0 146.9 jit_solution(11773797440149905769)
XLA Ops:
  0.0 4.0 %collective-permute-start.8 = (bf16[16,256,128]{2,1,0:T(8,128)(2,1)}, bf16[16,256,128]{2,1,0:T(8,128)(2,1)S(1)}, u32[]{:S(2)}, u32[]{:S(2)}) collective-permute-start(bf16[16,256,128]{2,1,0:T(8,128)(2,1)} %param.10), channel_id=1, source_target_pairs={{0,8},{1,9},{2,10},{3,11},{4,12},{5,13},{6,14},{7,15},{8,0},{9,1},... | collective-permute-start | bytes 3145736 | tf_op jit(solution)/shard_map/ppermute | solution.py:102
  4.0 1.6 %convert_reduce_fusion.3 = f32[16,256]{1,0:T(8,128)S(1)} fusion(bf16[16,256,128]{2,1,0:T(8,128)(2,1)} %param.10), kind=kLoop, calls=%fused_computation.8 | loop fusion | flops 1044480 | bytes 1064960 | tf_op jit(solution)/shard_map/reduce_sum | solution.py:14
  5.7 0.7 multiply_exponential_fusion.1
  6.6 0.7 convert_element_type.89
  7.3 0.7 multiply_exponential_fusion
  8.2 2.3 %fusion.28 = f32[16,256]{1,0:T(8,128)S(1)} fusion(bf16[16,256,128]{2,1,0:T(8,128)(2,1)} %param.10, f32[16,256]{1,0:T(8,128)S(1)} %broadcast_multiply_fusion.5), kind=kLoop, calls=%fused_computation.39 | loop fusion | flops 2093056 | bytes 1081344 | tf_op jit(solution)/shard_map/reduce_sum | solution.py:16
  10.7 39.2 %collective-permute-done.8 = bf16[16,256,128]{2,1,0:T(8,128)(2,1)S(1)} collective-permute-done((bf16[16,256,128]{2,1,0:T(8,128)(2,1)}, bf16[16,256,128]{2,1,0:T(8,128)(2,1)S(1)}, u32[]{:S(2)}, u32[]{:S(2)}) %collective-permute-start.8) | collective-permute-done | bytes 1048608 | tf_op jit(solution)/shard_map/ppermute | solution.py:102
  50.2 1.3 fusion.20
  51.6 2.5 %fusion.23 = (bf16[16,256,128]{2,1,0:T(8,128)(2,1)S(1)}, bf16[16,256,128]{2,1,0:T(8,128)(2,1)S(1)}) fusion(bf16[16,256,128]{2,1,0:T(8,128)(2,1)S(1)} %collective-permute-done.8, f32[16,256]{1,0:T(8,128)S(1)} %add_rsqrt_fusion.1, f32[16,256]{1,0:T(8,128)S(1)} %broadcast_multiply_fusion.4, f32[128]{0:T(128)S(1)} %copy-done.12, f32[128]{0:T(128)S(1)} %copy-done.13, ...), kind=kLoop, calls=%fused_computation.34 | loop fusion | flops 6291456 | bytes 4260864 | tf_op jit(solution)/shard_map/convert_element_type | solution.py:113
  54.1 0.7 fusion.54
  54.8 0.7 fusion.52
  55.5 2.0 %fusion.50 = (bf16[128,16,256]{0,2,1:T(8,128)(2,1)S(1)}, bf16[128,16,256]{0,2,1:T(8,128)(2,1)}) fusion(f32[16,256]{1,0:T(8,128)S(1)} %get-tuple-element.22, f32[16,256,256]{2,1,0:T(8,128)S(1)} %fusion.54, f32[16,256,256]{2,1,0:T(8,128)S(1)} %fusion.52), kind=kLoop, calls=%fused_computation.73 | loop fusion | flops 6291456 | bytes 10502144 | tf_op jit(solution)/shard_map/transpose | solution.py:79
  57.5 0.8 collective-permute-start
  58.3 1.5 %collective-permute-start.1 = (bf16[128,16,256]{0,2,1:T(8,128)(2,1)}, bf16[128,16,256]{0,2,1:T(8,128)(2,1)}, u32[]{:S(2)}, u32[]{:S(2)}) collective-permute-start(bf16[128,16,256]{0,2,1:T(8,128)(2,1)} %get-tuple-element.18), channel_id=1, source_target_pairs={{0,2},{1,3},{2,0},{3,1},{4,6},{5,7},{6,4},{7,5},{8,10},{9,11},{10,... | collective-permute-start | bytes 3145736 | tf_op jit(solution)/shard_map/ppermute | solution.py:102
  59.9 0.7 fusion.53
  61.2 0.9 copy.37
  62.1 0.7 fusion.51
  62.8 0.6 collective-permute-start.9
  63.8 18.3 %collective-permute-done = bf16[128,16,256]{0,2,1:T(8,128)(2,1)} collective-permute-done((bf16[128,16,256]{0,2,1:T(8,128)(2,1)}, bf16[128,16,256]{0,2,1:T(8,128)(2,1)}, u32[]{:S(2)}, u32[]{:S(2)}) %collective-permute-start) | collective-permute-done | bytes 1048608 | tf_op jit(solution)/shard_map/ppermute | solution.py:102
  82.2 1.3 collective-permute-start.2
  84.0 0.9 copy.35
  84.9 0.9 copy.36
  85.8 1.5 %pad_maximum_fusion.2 = bf16[128,32,256]{0,2,1:T(8,128)(2,1)} fusion(bf16[128,16,256]{0,2,1:T(8,128)(2,1)S(1)} %collective-permute-done.9, bf16[128,16,256]{0,2,1:T(8,128)(2,1)S(1)} %fusion.51), kind=kLoop, calls=%fused_computation.65 | loop fusion | flops 1048576 | bytes 4194304 | tf_op jit(solution)/shard_map/concatenate | solution.py:141
  87.3 3.4 %copy.23 = bf16[128,32,256]{2,1,0:T(8,128)(2,1)S(1)} copy(bf16[128,32,256]{0,2,1:T(8,128)(2,1)} %pad_maximum_fusion.2) | data formatting | bytes 4194304 | tf_op jit(solution)/shard_map/concatenate | solution.py:141
  90.7 2.8 %pad_maximum_fusion.1 = bf16[128,32,256]{0,2,1:T(8,128)(2,1)} fusion(bf16[128,16,256]{0,2,1:T(8,128)(2,1)} %collective-permute-done.3, bf16[128,16,256]{0,2,1:T(8,128)(2,1)S(1)} %get-tuple-element.17), kind=kLoop, calls=%fused_computation.64 | loop fusion | flops 1048576 | bytes 4194304 | tf_op jit(solution)/shard_map/concatenate | solution.py:141
  93.5 4.6 %copy.18 = bf16[128,32,256]{2,1,0:T(8,128)(2,1)} copy(bf16[128,32,256]{0,2,1:T(8,128)(2,1)} %pad_maximum_fusion.1) | data formatting | bytes 4194304 | tf_op jit(solution)/shard_map/concatenate | solution.py:141
  98.1 7.8 %collective-permute-done.2 = bf16[128,16,256]{0,2,1:T(8,128)(2,1)} collective-permute-done((bf16[128,16,256]{0,2,1:T(8,128)(2,1)}, bf16[128,16,256]{0,2,1:T(8,128)(2,1)}, u32[]{:S(2)}, u32[]{:S(2)}) %collective-permute-start.2) | collective-permute-done | bytes 1048608 | tf_op jit(solution)/shard_map/ppermute | solution.py:102
  105.9 3.8 %pad_maximum_fusion = bf16[128,64,256]{0,2,1:T(8,128)(2,1)} fusion(bf16[128,16,256]{0,2,1:T(8,128)(2,1)} %collective-permute-done.2, bf16[128,16,256]{0,2,1:T(8,128)(2,1)} %collective-permute-done.1, bf16[128,16,256]{0,2,1:T(8,128)(2,1)} %collective-permute-done, bf16[128,16,256]{0,2,1:T(8,128)(2,1)} %get-tuple-element.18), kind=kLoop, calls=%fused_computation | loop fusion | flops 6291456 | bytes 8388608 | tf_op jit(solution)/shard_map/concatenate | solution.py:136
  109.7 6.8 %copy.17 = bf16[128,64,256]{2,1,0:T(8,128)(2,1)} copy(bf16[128,64,256]{0,2,1:T(8,128)(2,1)} %pad_maximum_fusion) | data formatting | bytes 8388608 | tf_op jit(solution)/shard_map/concatenate | solution.py:136
  116.5 3.6 %convert_reduce_fusion = (f32[64,32]{0,1:T(8,128)S(1)}, bf16[128,64,32]{1,2,0:T(8,128)(2,1)S(1)}) fusion(bf16[128,64,256]{2,1,0:T(8,128)(2,1)} %copy.17, bf16[128,32,256]{2,1,0:T(8,128)(2,1)S(1)} %copy.23), kind=kOutput, calls=%fused_computation.2 | convolution fusion | flops 135002112 | bytes 6823936 | tf_op jit(solution)/shard_map/hjk,hik->hji/dot_general | solution.py:143
  120.1 0.5 copy-done.2
  120.7 1.2 convert_reduce_fusion.2
  122.7 0.9 fusion.19
  123.6 1.5 %copy.19 = bf16[128,64,32]{0,2,1:T(8,128)(2,1)S(1)} copy(bf16[128,64,32]{1,2,0:T(8,128)(2,1)S(1)} %get-tuple-element.20) | data formatting | bytes 1048576 | tf_op jit(solution)/shard_map/convert_element_type | solution.py:148
  125.2 1.3 fusion.48
  126.5 0.7 fusion.68
  127.2 2.4 %collective-permute-start.5 = (bf16[16,32,128]{2,1,0:T(8,128)(2,1)S(1)}, bf16[16,32,128]{2,1,0:T(8,128)(2,1)S(1)}, u32[]{:S(2)}, u32[]{:S(2)}) collective-permute-start(bf16[16,32,128]{2,1,0:T(8,128)(2,1)S(1)} %get-tuple-element.13), channel_id=1, source_target_pairs={{0,4},{1,5},{2,6},{3,7},{4,0},{5,1},{6,2},{7,3},{8,12},{9,13},{10,... | collective-permute-start | bytes 393224 | tf_op jit(solution)/shard_map/ppermute | solution.py:102
  129.5 1.5 %collective-permute-start.6 = (bf16[16,32,128]{2,1,0:T(8,128)(2,1)S(1)}, bf16[16,32,128]{2,1,0:T(8,128)(2,1)S(1)}, u32[]{:S(2)}, u32[]{:S(2)}) collective-permute-start(bf16[16,32,128]{2,1,0:T(8,128)(2,1)S(1)} %get-tuple-element.12), channel_id=1, source_target_pairs={{0,2},{1,3},{2,0},{3,1},{4,6},{5,7},{6,4},{7,5},{8,10},{9,11},{10,... | collective-permute-start | bytes 393224 | tf_op jit(solution)/shard_map/ppermute | solution.py:102
  131.1 1.5 %copy.24 = bf16[128,64,32]{0,2,1:T(8,128)(2,1)S(1)} copy(bf16[128,64,32]{1,2,0:T(8,128)(2,1)S(1)} %get-tuple-element.19) | data formatting | bytes 1048576 | tf_op jit(solution)/shard_map/convert_element_type | solution.py:148
  132.6 1.2 fusion.47
  133.9 0.7 fusion.66
  134.6 2.0 %collective-permute-start.11 = (bf16[16,32,128]{2,1,0:T(8,128)(2,1)S(1)}, bf16[16,32,128]{2,1,0:T(8,128)(2,1)S(1)}, u32[]{:S(2)}, u32[]{:S(2)}) collective-permute-start(bf16[16,32,128]{2,1,0:T(8,128)(2,1)S(1)} %get-tuple-element.7), channel_id=1, source_target_pairs={{0,4},{1,5},{2,6},{3,7},{4,0},{5,1},{6,2},{7,3},{8,12},{9,13},{10,... | collective-permute-start | bytes 393224 | tf_op jit(solution)/shard_map/ppermute | solution.py:102
  136.5 1.5 %collective-permute-start.12 = (bf16[16,32,128]{2,1,0:T(8,128)(2,1)S(1)}, bf16[16,32,128]{2,1,0:T(8,128)(2,1)S(1)}, u32[]{:S(2)}, u32[]{:S(2)}) collective-permute-start(bf16[16,32,128]{2,1,0:T(8,128)(2,1)S(1)} %get-tuple-element.6), channel_id=1, source_target_pairs={{0,2},{1,3},{2,0},{3,1},{4,6},{5,7},{6,4},{7,5},{8,10},{9,11},{10,... | collective-permute-start | bytes 393224 | tf_op jit(solution)/shard_map/ppermute | solution.py:102
  138.1 2.2 %collective-permute-done.11.refs_5_ = bf16[16,32,128]{2,1,0:T(8,128)(2,1)S(1)} collective-permute-done((bf16[16,32,128]{2,1,0:T(8,128)(2,1)S(1)}, bf16[16,32,128]{2,1,0:T(8,128)(2,1)S(1)}, u32[]{:S(2)}, u32[]{:S(2)}) %collective-permute-start.11) | collective-permute-done | bytes 131104 | tf_op jit(solution)/shard_map/ppermute | solution.py:102
  140.3 1.5 %collective-permute-done.12.refs_6_ = bf16[16,32,128]{2,1,0:T(8,128)(2,1)S(1)} collective-permute-done((bf16[16,32,128]{2,1,0:T(8,128)(2,1)S(1)}, bf16[16,32,128]{2,1,0:T(8,128)(2,1)S(1)}, u32[]{:S(2)}, u32[]{:S(2)}) %collective-permute-start.12) | collective-permute-done | bytes 131104 | tf_op jit(solution)/shard_map/ppermute | solution.py:102
  141.8 2.1 %collective-permute-done.13.refs_7_ = bf16[16,32,128]{2,1,0:T(8,128)(2,1)S(1)} collective-permute-done((bf16[16,32,128]{2,1,0:T(8,128)(2,1)S(1)}, bf16[16,32,128]{2,1,0:T(8,128)(2,1)S(1)}, u32[]{:S(2)}, u32[]{:S(2)}) %collective-permute-start.13) | collective-permute-done | bytes 131104 | tf_op jit(solution)/shard_map/ppermute | solution.py:102
  143.9 0.6 copy-done.10
  144.5 2.4 %shard_map.100 = bf16[16,256,128]{2,1,0:T(8,128)(2,1)} custom-call(bf16[16,32,128]{2,1,0:T(8,128)(2,1)} %get-tuple-element.14.refs_0_, bf16[16,32,128]{2,1,0:T(8,128)(2,1)} %copy-done.5, bf16[16,32,128]{2,1,0:T(8,128)(2,1)} %copy-done.6, bf16[16,32,128]{2,1,0:T(8,128)(2,1)} %copy-done.7, bf16[16,32,128]{2,1,0:T(8,128)(2,1)} %get-tuple-element.8.refs_4_, ...), custom_call_target="tpu_custom_call" | custom-call | tf_op jit(solution)/shard_map/pallas_call | solution.py:155
  (80 shorter events, 3.3 us)
Async XLA Ops:
  0.0 10.6 %copy-start.4 = (bf16[128,640]{1,0:T(8,128)(2,1)S(1)}, bf16[128,640]{1,0:T(8,128)(2,1)}, u32[]{:S(2)}) copy-start(bf16[128,640]{1,0:T(8,128)(2,1)} %param.12) | copy-start | bytes 491524
  0.0 49.9 %collective-permute-start.8 = (bf16[16,256,128]{2,1,0:T(8,128)(2,1)}, bf16[16,256,128]{2,1,0:T(8,128)(2,1)S(1)}, u32[]{:S(2)}, u32[]{:S(2)}) collective-permute-start(bf16[16,256,128]{2,1,0:T(8,128)(2,1)} %param.10), channel_id=1, source_target_pairs={{0,8},{1,9},{2,10},{3,11},{4,12},{5,13},{6,14},{7,15},{8,0},{9,1},... | collective-permute-start | bytes 3145736 | tf_op jit(solution)/shard_map/ppermute | solution.py:102
  5.6 45.9 %copy-start.1 = (bf16[16,256,128]{2,1,0:T(8,128)(2,1)S(1)}, bf16[16,256,128]{2,1,0:T(8,128)(2,1)}, u32[]{:S(2)}) copy-start(bf16[16,256,128]{2,1,0:T(8,128)(2,1)} %param.10) | copy-start | bytes 3145732
  5.7 45.9 %copy-start.12 = (f32[128]{0:T(128)S(1)}, f32[128]{0:T(128)}, u32[]{:S(2)}) copy-start(f32[128]{0:T(128)} %param.17) | copy-start | bytes 1540
  5.7 45.9 %copy-start.13 = (f32[128]{0:T(128)S(1)}, f32[128]{0:T(128)}, u32[]{:S(2)}) copy-start(f32[128]{0:T(128)} %param.16) | copy-start | bytes 1540
  57.5 24.7 %collective-permute-start = (bf16[128,16,256]{0,2,1:T(8,128)(2,1)}, bf16[128,16,256]{0,2,1:T(8,128)(2,1)}, u32[]{:S(2)}, u32[]{:S(2)}) collective-permute-start(bf16[128,16,256]{0,2,1:T(8,128)(2,1)} %get-tuple-element.18), channel_id=1, source_target_pairs={{0,4},{1,5},{2,6},{3,7},{4,0},{5,1},{6,2},{7,3},{8,12},{9,13},{10,... | collective-permute-start | bytes 3145736 | tf_op jit(solution)/shard_map/ppermute | solution.py:102
  58.3 39.8 %collective-permute-start.1 = (bf16[128,16,256]{0,2,1:T(8,128)(2,1)}, bf16[128,16,256]{0,2,1:T(8,128)(2,1)}, u32[]{:S(2)}, u32[]{:S(2)}) collective-permute-start(bf16[128,16,256]{0,2,1:T(8,128)(2,1)} %get-tuple-element.18), channel_id=1, source_target_pairs={{0,2},{1,3},{2,0},{3,1},{4,6},{5,7},{6,4},{7,5},{8,10},{9,11},{10,... | collective-permute-start | bytes 3145736 | tf_op jit(solution)/shard_map/ppermute | solution.py:102
  62.1 63.0 %collective-permute-start.4 = (bf16[16,64,128]{2,0,1:T(8,128)(2,1)}, bf16[16,64,128]{2,0,1:T(8,128)(2,1)}, u32[]{:S(2)}, u32[]{:S(2)}) collective-permute-start(bf16[16,64,128]{2,0,1:T(8,128)(2,1)} %bitcast.54), channel_id=1, source_target_pairs={{0,1},{1,0},{2,3},{3,2},{4,5},{5,4},{6,7},{7,6},{8,9},{9,8},{10,11... | collective-permute-start | bytes 786440 | tf_op jit(solution)/shard_map/ppermute | solution.py:102
  62.8 22.9 %collective-permute-start.9 = (bf16[128,16,256]{0,2,1:T(8,128)(2,1)S(1)}, bf16[128,16,256]{0,2,1:T(8,128)(2,1)S(1)}, u32[]{:S(2)}, u32[]{:S(2)}) collective-permute-start(bf16[128,16,256]{0,2,1:T(8,128)(2,1)S(1)} %fusion.51), channel_id=1, source_target_pairs={{0,1},{1,0},{2,3},{3,2},{4,5},{5,4},{6,7},{7,6},{8,9},{9,8},{10,11... | collective-permute-start | bytes 3145736 | tf_op jit(solution)/shard_map/ppermute | solution.py:102
  63.4 27.3 %collective-permute-start.3 = (bf16[128,16,256]{0,2,1:T(8,128)(2,1)S(1)}, bf16[128,16,256]{0,2,1:T(8,128)(2,1)}, u32[]{:S(2)}, u32[]{:S(2)}) collective-permute-start(bf16[128,16,256]{0,2,1:T(8,128)(2,1)S(1)} %get-tuple-element.17), channel_id=1, source_target_pairs={{0,1},{1,0},{2,3},{3,2},{4,5},{5,4},{6,7},{7,6},{8,9},{9,8},{10,11... | collective-permute-start | bytes 3145736 | tf_op jit(solution)/shard_map/ppermute | solution.py:102
  82.2 23.8 %collective-permute-start.2 = (bf16[128,16,256]{0,2,1:T(8,128)(2,1)}, bf16[128,16,256]{0,2,1:T(8,128)(2,1)}, u32[]{:S(2)}, u32[]{:S(2)}) collective-permute-start(bf16[128,16,256]{0,2,1:T(8,128)(2,1)} %collective-permute-done), channel_id=1, source_target_pairs={{0,2},{1,3},{2,0},{3,1},{4,6},{5,7},{6,4},{7,5},{8,10},{9,11},{10,... | collective-permute-start | bytes 3145736 | tf_op jit(solution)/shard_map/ppermute | solution.py:102
  85.8 46.8 %collective-permute-start.10 = (bf16[16,64,128]{2,0,1:T(8,128)(2,1)}, bf16[16,64,128]{2,0,1:T(8,128)(2,1)}, u32[]{:S(2)}, u32[]{:S(2)}) collective-permute-start(bf16[16,64,128]{2,0,1:T(8,128)(2,1)} %bitcast.52), channel_id=1, source_target_pairs={{0,1},{1,0},{2,3},{3,2},{4,5},{5,4},{6,7},{7,6},{8,9},{9,8},{10,11... | collective-permute-start | bytes 786440 | tf_op jit(solution)/shard_map/ppermute | solution.py:102
  116.5 3.6 %copy-start = (bf16[128,64,256]{2,1,0:T(8,128)(2,1)S(1)}, bf16[128,64,256]{2,1,0:T(8,128)(2,1)}, u32[]{:S(2)}) copy-start(bf16[128,64,256]{2,1,0:T(8,128)(2,1)} %copy.17) | copy-start | bytes 12582916
  116.5 4.1 %copy-start.2 = (bf16[128,32,256]{2,1,0:T(8,128)(2,1)S(1)}, bf16[128,32,256]{2,1,0:T(8,128)(2,1)}, u32[]{:S(2)}) copy-start(bf16[128,32,256]{2,1,0:T(8,128)(2,1)} %copy.18) | copy-start | bytes 6291460
  121.9 0.8 copy-start.14
  121.9 0.8 copy-start.15
  122.7 2.5 %copy-start.11 = (bf16[128,128]{1,0:T(8,128)(2,1)S(1)}, bf16[128,128]{1,0:T(8,128)(2,1)}, u32[]{:S(2)}) copy-start(bf16[128,128]{1,0:T(8,128)(2,1)} %param.14) | copy-start | bytes 98308
  125.2 7.5 %copy-start.3 = (bf16[16,1,64,128]{3,0,2,1:T(8,128)(2,1)S(1)}, bf16[16,1,64,128]{3,0,2,1:T(8,128)(2,1)}, u32[]{:S(2)}) copy-start(bf16[16,1,64,128]{3,0,2,1:T(8,128)(2,1)} %copy.36) | copy-start | bytes 786436
  127.2 10.9 %collective-permute-start.5 = (bf16[16,32,128]{2,1,0:T(8,128)(2,1)S(1)}, bf16[16,32,128]{2,1,0:T(8,128)(2,1)S(1)}, u32[]{:S(2)}, u32[]{:S(2)}) collective-permute-start(bf16[16,32,128]{2,1,0:T(8,128)(2,1)S(1)} %get-tuple-element.13), channel_id=1, source_target_pairs={{0,4},{1,5},{2,6},{3,7},{4,0},{5,1},{6,2},{7,3},{8,12},{9,13},{10,... | collective-permute-start | bytes 393224 | tf_op jit(solution)/shard_map/ppermute | solution.py:102
  129.5 8.5 %collective-permute-start.6 = (bf16[16,32,128]{2,1,0:T(8,128)(2,1)S(1)}, bf16[16,32,128]{2,1,0:T(8,128)(2,1)S(1)}, u32[]{:S(2)}, u32[]{:S(2)}) collective-permute-start(bf16[16,32,128]{2,1,0:T(8,128)(2,1)S(1)} %get-tuple-element.12), channel_id=1, source_target_pairs={{0,2},{1,3},{2,0},{3,1},{4,6},{5,7},{6,4},{7,5},{8,10},{9,11},{10,... | collective-permute-start | bytes 393224 | tf_op jit(solution)/shard_map/ppermute | solution.py:102
  131.0 7.0 %collective-permute-start.7 = (bf16[16,32,128]{2,1,0:T(8,128)(2,1)S(1)}, bf16[16,32,128]{2,1,0:T(8,128)(2,1)S(1)}, u32[]{:S(2)}, u32[]{:S(2)}) collective-permute-start(bf16[16,32,128]{2,1,0:T(8,128)(2,1)S(1)} %get-tuple-element.11), channel_id=1, source_target_pairs={{0,6},{1,7},{2,4},{3,5},{4,2},{5,3},{6,0},{7,1},{8,14},{9,15},{10,... | collective-permute-start | bytes 393224 | tf_op jit(solution)/shard_map/ppermute | solution.py:102
  134.6 5.7 %collective-permute-start.11 = (bf16[16,32,128]{2,1,0:T(8,128)(2,1)S(1)}, bf16[16,32,128]{2,1,0:T(8,128)(2,1)S(1)}, u32[]{:S(2)}, u32[]{:S(2)}) collective-permute-start(bf16[16,32,128]{2,1,0:T(8,128)(2,1)S(1)} %get-tuple-element.7), channel_id=1, source_target_pairs={{0,4},{1,5},{2,6},{3,7},{4,0},{5,1},{6,2},{7,3},{8,12},{9,13},{10,... | collective-permute-start | bytes 393224 | tf_op jit(solution)/shard_map/ppermute | solution.py:102
  136.5 5.2 %collective-permute-start.12 = (bf16[16,32,128]{2,1,0:T(8,128)(2,1)S(1)}, bf16[16,32,128]{2,1,0:T(8,128)(2,1)S(1)}, u32[]{:S(2)}, u32[]{:S(2)}) collective-permute-start(bf16[16,32,128]{2,1,0:T(8,128)(2,1)S(1)} %get-tuple-element.6), channel_id=1, source_target_pairs={{0,2},{1,3},{2,0},{3,1},{4,6},{5,7},{6,4},{7,5},{8,10},{9,11},{10,... | collective-permute-start | bytes 393224 | tf_op jit(solution)/shard_map/ppermute | solution.py:102
  138.0 5.9 %copy-start.5 = (bf16[16,32,128]{2,1,0:T(8,128)(2,1)}, bf16[16,32,128]{2,1,0:T(8,128)(2,1)S(1)}, u32[]{:S(2)}) copy-start(bf16[16,32,128]{2,1,0:T(8,128)(2,1)S(1)} %collective-permute-done.5.refs_1_) | copy-start | bytes 393220
  138.0 5.9 %collective-permute-start.13 = (bf16[16,32,128]{2,1,0:T(8,128)(2,1)S(1)}, bf16[16,32,128]{2,1,0:T(8,128)(2,1)S(1)}, u32[]{:S(2)}, u32[]{:S(2)}) collective-permute-start(bf16[16,32,128]{2,1,0:T(8,128)(2,1)S(1)} %get-tuple-element.5), channel_id=1, source_target_pairs={{0,6},{1,7},{2,4},{3,5},{4,2},{5,3},{6,0},{7,1},{8,14},{9,15},{10,... | collective-permute-start | bytes 393224 | tf_op jit(solution)/shard_map/ppermute | solution.py:102
  138.1 5.9 %copy-start.6 = (bf16[16,32,128]{2,1,0:T(8,128)(2,1)}, bf16[16,32,128]{2,1,0:T(8,128)(2,1)S(1)}, u32[]{:S(2)}) copy-start(bf16[16,32,128]{2,1,0:T(8,128)(2,1)S(1)} %collective-permute-done.6.refs_2_) | copy-start | bytes 393220
  138.1 5.8 %copy-start.7 = (bf16[16,32,128]{2,1,0:T(8,128)(2,1)}, bf16[16,32,128]{2,1,0:T(8,128)(2,1)S(1)}, u32[]{:S(2)}) copy-start(bf16[16,32,128]{2,1,0:T(8,128)(2,1)S(1)} %collective-permute-done.7.refs_3_) | copy-start | bytes 393220
  140.3 3.7 %copy-start.8 = (bf16[16,32,128]{2,1,0:T(8,128)(2,1)}, bf16[16,32,128]{2,1,0:T(8,128)(2,1)S(1)}, u32[]{:S(2)}) copy-start(bf16[16,32,128]{2,1,0:T(8,128)(2,1)S(1)} %collective-permute-done.11.refs_5_) | copy-start | bytes 393220
  141.8 2.2 %copy-start.9 = (bf16[16,32,128]{2,1,0:T(8,128)(2,1)}, bf16[16,32,128]{2,1,0:T(8,128)(2,1)S(1)}, u32[]{:S(2)}) copy-start(bf16[16,32,128]{2,1,0:T(8,128)(2,1)S(1)} %collective-permute-done.12.refs_6_) | copy-start | bytes 393220
  143.9 0.6 copy-start.10

commit v2 on v0

--- a/solution.py
+++ b/solution.py
@@ -1,6 +1,10 @@
+import functools
+
 import jax
 import jax.numpy as jnp
 from jax import lax
+from jax.experimental import pallas as pl
+from jax.experimental.pallas import tpu as pltpu
 from jax.sharding import PartitionSpec as P
 
 BLK = 32
@@ -62,9 +66,290 @@
     return (mixed * gate_cols.astype(jnp.float32)).astype(jnp.bfloat16)
 
 
+CORE, Y, Z, HALF = 1, 2, 4, 8
+CHIPS = (0, Z, Y, Z | Y)
+FAR_CHUNKS = 4
+RIGHT_CHUNKS = 4
+
+
+def other(me, bits):
+    for bit in (CORE, Y, Z, HALF):
+        if bits & bit:
+            me = me + bit * (1 - 2 * ((me // bit) % 2))
+    return me
+
+
+def sigmoid(values):
+    return 0.5 + 0.5 * jnp.tanh(0.5 * values)
+
+
+def triangle(
+    rows,
+    whole_len,
+    hidden,
+    pair_ref,
+    mask_ref,
+    side_w_ref,
+    gate_w_ref,
+    last_w_ref,
+    in_gain_ref,
+    in_bias_ref,
+    out_gain_ref,
+    out_bias_ref,
+    out_ref,
+    far_ref,
+    norm_ref,
+    stage_ref,
+    gate_stage_ref,
+    right_ref,
+    left_ref,
+    gate_ref,
+    gate_send_ref,
+    tri_ref,
+    update_ref,
+    send_sem,
+    recv_sem,
+):
+    me = lax.axis_index("ia")
+    barrier = pltpu.get_barrier_semaphore()
+    peers = (CORE, Y, Z, Z | Y, HALF)
+    for bits in peers:
+        pl.semaphore_signal(
+            barrier, inc=1, device_id={"ia": other(me, bits)}, device_id_type=pl.DeviceIdType.MESH
+        )
+    pl.semaphore_wait(barrier, len(peers))
+
+    started = []
+
+    def send(src, dst, bits):
+        at = len(started)
+        copy = pltpu.make_async_remote_copy(
+            src_ref=src,
+            dst_ref=dst,
+            send_sem=send_sem.at[at],
+            recv_sem=recv_sem.at[at],
+            device_id={"ia": other(me, bits)},
+            device_id_type=pl.DeviceIdType.MESH,
+        )
+        copy.start()
+        started.append(copy)
+        return copy
+
+    far_rows = rows // FAR_CHUNKS
+    far_copies = []
+    for at in range(FAR_CHUNKS):
+        part = pl.ds(at * far_rows, far_rows)
+        far_copies.append(send(pair_ref.at[part], far_ref.at[part], HALF))
+
+    contract_last = (((1,), (1,)), ((), ()))
+    contract_first = (((0,), (0,)), ((), ()))
+
+    def normalise(src_ref, row):
+        values = src_ref[row].astype(jnp.float32)
+        normed = layer_norm(values, in_gain_ref[...], in_bias_ref[...], -1)
+        norm_ref[row] = normed.astype(jnp.bfloat16)
+
+    def project(row, side, mask_row):
+        weight = side_w_ref[side * 2 * hidden : (side + 1) * 2 * hidden, :]
+        proj = lax.dot_general(
+            weight, norm_ref[row], contract_last, preferred_element_type=jnp.float32
+        )
+        value = sigmoid(proj[:hidden]) * proj[hidden:] * mask_ref[mask_row]
+        for lane in range(whole_len // 128):
+            stage_ref[lane, pl.ds(row, hidden, stride=rows), :] = value[
+                :, lane * 128 : (lane + 1) * 128
+            ]
+
+    def unstage(dst_ref, slot, start, size):
+        for lane in range(whole_len // 128):
+            dst_ref[slot, start : start + size, :, lane * 128 : (lane + 1) * 128] = (
+                stage_ref[lane, start * rows : (start + size) * rows, :]
+                .reshape(size, rows, 128)
+                .astype(jnp.bfloat16)
+            )
+
+    @pl.loop(0, rows)
+    def _(row):
+        normalise(pair_ref, row)
+        project(row, 1, row)
+
+    part_size = hidden // RIGHT_CHUNKS
+    z_copies, y_copies = [], []
+    for at in range(RIGHT_CHUNKS):
+        unstage(right_ref, 0, at * part_size, part_size)
+        part = pl.ds(at * part_size, part_size)
+        z_copies.append(send(right_ref.at[0, part], right_ref.at[1, part], Z))
+        y_copies.append(send(right_ref.at[0, part], right_ref.at[2, part], Y))
+
+    gate_cols = [
+        pl.ds(pl.multiple_of(other(me, core | chip) * rows, rows), rows)
+        for core in (0, CORE)
+        for chip in CHIPS
+    ]
+    cols = rows * len(CHIPS)
+
+    def gates(row):
+        picked = jnp.concatenate([norm_ref[row, part, :] for part in gate_cols], 0)
+        gate = sigmoid(jnp.dot(picked, gate_w_ref[...], preferred_element_type=jnp.float32))
+        gate_stage_ref[pl.ds(row, 2 * cols, stride=rows), :] = gate
+
+    def finish_rows(slot):
+        unstage(left_ref, slot, 0, hidden)
+        gate_ref[slot] = (
+            gate_stage_ref[0 : cols * rows, :].reshape(cols, rows, hidden).astype(jnp.bfloat16)
+        )
+        gate_send_ref[slot // 2] = (
+            gate_stage_ref[cols * rows :, :].reshape(cols, rows, hidden).astype(jnp.bfloat16)
+        )
+        return [
+            send(left_ref.at[slot], left_ref.at[slot + 1], CORE),
+            send(gate_send_ref.at[slot // 2], gate_ref.at[slot + 1], CORE),
+        ]
+
+    @pl.loop(0, rows)
+    def _(row):
+        project(row, 0, row)
+        gates(row)
+
+    core_copies = finish_rows(0)
+    forward = []
+
+    def pass_on(at):
+        z_copies[at].wait_recv()
+        part = pl.ds(at * part_size, part_size)
+        forward.append(send(right_ref.at[1, part], right_ref.at[3, part], Y))
+
+    for at in range(FAR_CHUNKS):
+        if at < RIGHT_CHUNKS:
+            pass_on(at)
+        far_copies[at].wait_recv()
+
+        @pl.loop(at * far_rows, (at + 1) * far_rows)
+        def _(row):
+            normalise(far_ref, row)
+            project(row, 0, rows + row)
+            gates(row)
+
+    core_copies += finish_rows(2)
+    for copy in core_copies + y_copies:
+        copy.wait_recv()
+
+    half_cols = cols // 2
+    for at in range(RIGHT_CHUNKS):
+        forward[at].wait_recv()
+
+        @pl.loop(at * part_size, (at + 1) * part_size, step=4)
+        def _(base):
+            for more in range(4):
+                chan = base + more
+                right = jnp.concatenate([right_ref[slot, chan] for slot in range(4)], 0)
+                left = jnp.concatenate([left_ref[slot, chan] for slot in range(4)], 0)
+                tri = lax.dot_general(
+                    right, left, contract_last, preferred_element_type=jnp.float32
+                )
+                tri = tri.astype(jnp.bfloat16).astype(jnp.float32)
+                start = pl.multiple_of(chan * half_cols, half_cols)
+                tri_ref[pl.ds(start, half_cols), :] = jnp.concatenate(
+                    [tri[:half_cols], tri[half_cols:]], 1
+                )
+
+    def finish_col(col):
+        tri = tri_ref[pl.ds(col, hidden, stride=half_cols), :]
+        normed = layer_norm(tri, out_gain_ref[...], out_bias_ref[...], 0).astype(jnp.bfloat16)
+        mixed = lax.dot_general(
+            normed, last_w_ref[...], contract_first, preferred_element_type=jnp.float32
+        )
+        for upper in range(2):
+            at = col + upper * half_cols
+            gate = jnp.concatenate([gate_ref[slot, at] for slot in range(4)], 0)
+            part = mixed[upper * cols : (upper + 1) * cols]
+            update_ref[at] = (part * gate.astype(jnp.float32)).astype(jnp.bfloat16)
+
+    blocks = (0, CORE, HALF, HALF | CORE)
+    places = [
+        pl.ds(pl.multiple_of(other(me, block) * rows, rows), rows) for block in blocks
+    ]
+    for low in (1, 0):
+
+        @pl.loop(low * rows, (low + 1) * rows)
+        def _(col):
+            finish_col(col)
+
+        for chip_at in (low + 2, low):
+            for at, place in enumerate(places):
+                src = update_ref.at[
+                    chip_at * rows : (chip_at + 1) * rows, at * rows : (at + 1) * rows, :
+                ]
+                if chip_at:
+                    send(src, out_ref.at[:, place, :], CHIPS[chip_at])
+                else:
+                    out_ref[:, place, :] = src[...]
+
+    for copy in started:
+        copy.wait_send()
+    for copy in started[-12:]:
+        copy.wait_recv()
+
+
+def half_shards(
+    pair, pad_mask, w_in, in_exps, w_out, out_exps, in_gain, in_bias, out_gain, out_bias
+):
+    rows, whole_len, _ = pair.shape
+    hidden = w_out.shape[0]
+    me = lax.axis_index("ia")
+    w_eff = scaled_weight(w_in, in_exps)
+    w_last = scaled_weight(w_out, out_exps)
+    mask_f = pad_mask.astype(jnp.float32)
+    mask_rows = jnp.concatenate(
+        [
+            lax.dynamic_slice_in_dim(mask_f, owner * rows, rows, 0)
+            for owner in (me, other(me, HALF))
+        ]
+    )
+    masks = mask_rows[:, None, None] * mask_f[None, None, :]
+    cols = 4 * rows
+    vmem = pl.BlockSpec(memory_space=pltpu.VMEM)
+    copies = FAR_CHUNKS + 3 * RIGHT_CHUNKS + 4 + 12
+    return pl.pallas_call(
+        functools.partial(triangle, rows, whole_len, hidden),
+        out_shape=jax.ShapeDtypeStruct(pair.shape, jnp.bfloat16),
+        in_specs=[vmem] * 9,
+        out_specs=vmem,
+        scratch_shapes=[
+            pltpu.VMEM(pair.shape, jnp.bfloat16),
+            pltpu.VMEM(pair.shape, jnp.bfloat16),
+            pltpu.VMEM((whole_len // 128, hidden * rows, 128), jnp.float32),
+            pltpu.VMEM((2 * cols * rows, hidden), jnp.float32),
+            pltpu.VMEM((4, hidden, rows, whole_len), jnp.bfloat16),
+            pltpu.VMEM((4, hidden, rows, whole_len), jnp.bfloat16),
+            pltpu.VMEM((4, cols, rows, hidden), jnp.bfloat16),
+            pltpu.VMEM((2, cols, rows, hidden), jnp.bfloat16),
+            pltpu.VMEM((hidden * cols // 2, 2 * cols), jnp.float32),
+            pltpu.VMEM((cols, cols, hidden), jnp.bfloat16),
+            pltpu.SemaphoreType.DMA((copies,)),
+            pltpu.SemaphoreType.DMA((copies,)),
+        ],
+        compiler_params=pltpu.CompilerParams(
+            collective_id=0, has_side_effects=True, vmem_limit_bytes=40 * 2**20
+        ),
+    )(
+        pair,
+        masks,
+        w_eff[:, : 4 * hidden].T,
+        w_eff[:, 4 * hidden :],
+        w_last,
+        in_gain[None, :],
+        in_bias[None, :],
+        out_gain[:, None],
+        out_bias[:, None],
+    )
+
+
 def solution(mesh):
+    count = mesh.shape["ia"]
+    body = half_shards if count == 16 else shards
     return jax.shard_map(
-        shards,
+        body,
         mesh=mesh,
         in_specs=(
             P(("groups", "ia"), None, None),

time: 137 us -> 94.2 us (0.69)
  Pallas kernels: 0 us -> 87 us
  waiting for transfers between devices: 85.8 us -> 0 us
  starting transfers between devices: 28 us -> 0 us
  other arithmetic: 9.18 us -> 3.09 us
  local copies, waits for them, and re-layouts: 8.48 us -> 3.54 us
  matrix products: 3.88 us -> 0 us
    pallas_call x0 -> x1, Pallas kernels: none -> 87 us  [half_shards(): pl.pallas_call(functools.partial(triangle, rows, whole_len, hidden), out_...]
    all_to_all x4 -> x0, waiting for transfers between devices: 85.8 us -> none  [the longest x1 22.6 us: shards(): lax.all_to_all(tri_t, 'ia', split_axis=1, concat_axis=0, tiled=True)]
    all_to_all x4 -> x0, starting transfers between devices: 28 us -> none  [the longest x1 7.4 us: shards(): lax.all_to_all(right_t, 'ia', split_axis=0, concat_axis=1, tiled=True)]
    reduce_sum x4 -> x0, other arithmetic: 4.44 us -> none  [the longest x2 2.66 us: layer_norm(): variance = jnp.mean(centred * centred, axis=axis, keepdims=True)]
    dot_general x3 -> x0, matrix products: 3.88 us -> none  [the longest x1 1.83 us: shards(): jnp.dot(normed.reshape(tok_rows * whole_len, width_in), w_eff, preferred_...]
    convert_element_type x4 -> x0, local copies, waits for them, and re-layouts: 3.71 us -> none  [the longest x1 1.65 us: shards(): jax.nn.sigmoid(proj[:, :, 4 * hidden:5 * hidden]).astype(jnp.bfloat16)]
    transpose x2, local copies, waits for them, and re-layouts: 3.4 us -> 0.13 us  [half_shards(): w_eff[:, :4 * hidden]]
    transpose x1 -> x0, other arithmetic: 1.95 us -> none  [shards(): left_t = jnp.transpose(left, (2, 0, 1))]
  transfers between devices with their start and end apart: 4 -> 0, of which waited for: 4 -> 0; matrix products, arithmetic and copies ran while one was open for 4% -> 0% of each run, Pallas kernels for 0% -> 0%
where the time goes in v2:
time: 94.2 us; the launch traced here: 93.7 us
  Pallas kernels  87 us (92%)
  local copies, waits for them, and re-layouts  3.54 us (4%)
  other arithmetic  3.09 us (3%)
    pallas_call x1, Pallas kernels, half_shards(): pl.pallas_call(functools.partial(triangle, rows, whole_len, hidden), out_...  87 us

profile of v2, /device:TPU:0, one launch (start us, length us, event | category | flops | bytes accessed | tf_op | source)
XLA Modules:
  0.0 93.7 jit_solution(7474593964737181809)
XLA Ops:
  0.0 0.0 copy-start.3
  0.0 0.0 copy-start
  0.0 0.8 multiply_exponential_fusion.1
  0.8 0.7 multiply_exponential_fusion
  1.4 0.7 convert_element_type.21
  2.1 0.1 fusion
  2.2 0.1 pad_maximum_fusion
  2.3 0.1 broadcast_in_dim.21
  2.3 0.1 mul.55
  2.4 0.1 broadcast_in_dim.20
  2.5 0.1 mul.52
  2.6 0.1 broadcast_multiply_fusion.mask_ref
  2.7 0.8 multiply_convert_fusion.1.last_w_ref
  3.5 0.8 copy.12.out_gain_ref
  4.2 0.8 copy.13.out_bias_ref
  5.0 0.0 copy-done.3
  5.1 0.0 copy-start.1
  5.1 0.0 copy-start.2
  5.1 0.1 copy.11.side_w_ref
  5.2 0.0 copy-done
  5.2 0.5 copy-done.1
  5.7 0.0 copy-done.2
  5.7 87.0 %shard_map.100 = bf16[16,256,128]{2,1,0:T(8,128)(2,1)S(1)} custom-call(bf16[16,256,128]{2,1,0:T(8,128)(2,1)S(1)} %copy-done, f32[32,1,256]{2,1,0:T(1,128)S(1)} %broadcast_multiply_fusion.mask_ref, bf16[512,128]{1,0:T(8,128)(2,1)S(1)} %copy.11.side_w_ref, bf16[128,128]{1,0:T(8,128)(2,1)S(1)} %slice.9.gate_w_ref, ...), custom_call_target="tpu_custom_call" | custom-call | tf_op jit(solution)/shard_map/pallas_call | solution.py:313
  92.7 1.0 %copy.15 = bf16[16,256,128]{2,1,0:T(8,128)(2,1)} copy(bf16[16,256,128]{2,1,0:T(8,128)(2,1)S(1)} %shard_map.100) | data formatting | bytes 2097152
  (3 shorter events, 0.0 us)
Async XLA Ops:
  0.0 5.0 %copy-start.3 = (bf16[128,640]{1,0:T(8,128)(2,1)S(1)}, bf16[128,640]{1,0:T(8,128)(2,1)}, u32[]{:S(2)}) copy-start(bf16[128,640]{1,0:T(8,128)(2,1)} %param.12) | copy-start | bytes 491524
  0.0 5.2 %copy-start = (bf16[16,256,128]{2,1,0:T(8,128)(2,1)S(1)}, bf16[16,256,128]{2,1,0:T(8,128)(2,1)}, u32[]{:S(2)}) copy-start(bf16[16,256,128]{2,1,0:T(8,128)(2,1)} %pair_ref.1) | copy-start | bytes 3145732
  5.1 0.7 copy-start.1
  5.1 0.7 copy-start.2

commit v3 on v2

--- a/solution.py
+++ b/solution.py
@@ -168,7 +168,7 @@
                 .astype(jnp.bfloat16)
             )
 
-    @pl.loop(0, rows)
+    @pl.loop(0, rows, unroll=4)
     def _(row):
         normalise(pair_ref, row)
         project(row, 1, row)
@@ -206,7 +206,7 @@
             send(gate_send_ref.at[slot // 2], gate_ref.at[slot + 1], CORE),
         ]
 
-    @pl.loop(0, rows)
+    @pl.loop(0, rows, unroll=4)
     def _(row):
         project(row, 0, row)
         gates(row)
@@ -224,7 +224,7 @@
             pass_on(at)
         far_copies[at].wait_recv()
 
-        @pl.loop(at * far_rows, (at + 1) * far_rows)
+        @pl.loop(at * far_rows, (at + 1) * far_rows, unroll=4)
         def _(row):
             normalise(far_ref, row)
             project(row, 0, rows + row)
@@ -235,6 +235,9 @@
         copy.wait_recv()
 
     half_cols = cols // 2
+    gain_col, bias_col = (
+        jnp.broadcast_to(ref[...], (2 * cols, hidden)).T for ref in (out_gain_ref, out_bias_ref)
+    )
     for at in range(RIGHT_CHUNKS):
         forward[at].wait_recv()
 
@@ -255,7 +258,7 @@
 
     def finish_col(col):
         tri = tri_ref[pl.ds(col, hidden, stride=half_cols), :]
-        normed = layer_norm(tri, out_gain_ref[...], out_bias_ref[...], 0).astype(jnp.bfloat16)
+        normed = layer_norm(tri, gain_col, bias_col, 0).astype(jnp.bfloat16)
         mixed = lax.dot_general(
             normed, last_w_ref[...], contract_first, preferred_element_type=jnp.float32
         )
@@ -271,7 +274,7 @@
     ]
     for low in (1, 0):
 
-        @pl.loop(low * rows, (low + 1) * rows)
+        @pl.loop(low * rows, (low + 1) * rows, unroll=4)
         def _(col):
             finish_col(col)
 
@@ -340,8 +343,8 @@
         w_last,
         in_gain[None, :],
         in_bias[None, :],
-        out_gain[:, None],
-        out_bias[:, None],
+        out_gain[None, :],
+        out_bias[None, :],
     )
 
 

time: 94.2 us -> 85.6 us (0.909)
  Pallas kernels: 87 us -> 78.8 us
  local copies, waits for them, and re-layouts: 3.54 us -> 2.02 us
    pallas_call x1, Pallas kernels: 87 us -> 78.8 us  [half_shards(): pl.pallas_call(functools.partial(triangle, rows, whole_len, hidden), out_...]
    broadcast_in_dim x2 -> x0, local copies, waits for them, and re-layouts: 1.52 us -> none  [the longest x1 0.76 us: half_shards(): out_gain[:, None]]
where the time goes in v3:
time: 85.6 us; the launch traced here: 84.9 us
  Pallas kernels  78.8 us (92%)
  other arithmetic  4 us (5%)
  local copies, waits for them, and re-layouts  2.02 us (2%)
    pallas_call x1, Pallas kernels, half_shards(): pl.pallas_call(functools.partial(triangle, rows, whole_len, hidden), out_...  78.8 us
    convert_element_type x2, other arithmetic, scaled_weight(): return (weight.astype(jnp.float32) * factor[None, :]).astype(jnp.bfloat16)  1.72 us

profile of v3, /device:TPU:0, one launch (start us, length us, event | category | flops | bytes accessed | tf_op | source)
XLA Modules:
  0.0 84.9 jit_solution(2132275613701257195)
XLA Ops:
  0.0 0.0 copy-start
  0.0 0.7 multiply_exponential_fusion.1
  0.8 0.7 multiply_exponential_fusion
  1.4 0.7 convert_element_type.21
  2.1 0.1 fusion
  2.2 0.1 pad_maximum_fusion
  2.3 0.1 broadcast_in_dim.21
  2.3 0.1 mul.55
  2.4 0.1 broadcast_in_dim.20
  2.5 0.1 mul.52
  2.6 0.1 broadcast_multiply_fusion.mask_ref
  2.7 0.8 multiply_convert_fusion.1.last_w_ref
  3.4 1.0 %multiply_convert_fusion = bf16[128,640]{1,0:T(8,128)(2,1)S(1)} fusion(bf16[128,640]{1,0:T(8,128)(2,1)} %param.12, f32[640]{0:T(1024)S(1)} %mul.52), kind=kLoop, calls=%fused_computation | loop fusion | flops 245760 | bytes 330240 | tf_op jit(solution)/shard_map/convert_element_type | solution.py:22
  4.4 0.0 copy-start.1
  4.4 0.0 copy-start.2
  4.4 0.0 copy-start.3
  4.5 0.0 copy-start.4
  4.5 0.1 copy.11.side_w_ref
  4.6 0.0 copy-done
  4.6 0.5 copy-done.1
  5.1 0.0 copy-done.2
  5.1 0.0 copy-done.3
  5.1 0.0 copy-done.4
  5.1 78.8 %shard_map.100 = bf16[16,256,128]{2,1,0:T(8,128)(2,1)S(1)} custom-call(bf16[16,256,128]{2,1,0:T(8,128)(2,1)S(1)} %copy-done, f32[32,1,256]{2,1,0:T(1,128)S(1)} %broadcast_multiply_fusion.mask_ref, bf16[512,128]{1,0:T(8,128)(2,1)S(1)} %copy.11.side_w_ref, bf16[128,128]{1,0:T(8,128)(2,1)S(1)} %slice.9.gate_w_ref, ...), custom_call_target="tpu_custom_call" | custom-call | tf_op jit(solution)/shard_map/pallas_call | solution.py:316
  83.9 1.0 %copy.13 = bf16[16,256,128]{2,1,0:T(8,128)(2,1)} copy(bf16[16,256,128]{2,1,0:T(8,128)(2,1)S(1)} %shard_map.100) | data formatting | bytes 2097152
  (2 shorter events, 0.0 us)
Async XLA Ops:
  0.0 4.6 %copy-start = (bf16[16,256,128]{2,1,0:T(8,128)(2,1)S(1)}, bf16[16,256,128]{2,1,0:T(8,128)(2,1)}, u32[]{:S(2)}) copy-start(bf16[16,256,128]{2,1,0:T(8,128)(2,1)} %pair_ref.1) | copy-start | bytes 3145732
  4.4 0.7 copy-start.1
  4.4 0.7 copy-start.2
  4.4 0.7 copy-start.3
  4.5 0.7 copy-start.4
